TPU v7x, 256 devices: a whole 4x4x8 slice. The times are simulated.
256 devices in a mesh: pole: 4 (over z_lo), prow: 8 (over x, core), pcol: 8 (over y, z_hi).
Axes of the slice: x: 4, y: 4, z: 8 (z_hi: 2, z_lo: 4; z = z_hi * 4 + z_lo), core: 2. Of those that a mesh axis runs over, the one named last changes fastest.
Arguments:
- lower: float32 [4, 4096, 4096], P('pole', 'prow', 'pcol'), may hold values from -0.1875 to 0.1875
- upper: float32 [4, 4096, 4096], P('pole', 'prow', 'pcol'), may hold values from -0.1875 to 0.1875
- dinv: float32 [4, 4096, 4096], P('pole', 'prow', 'pcol'), may hold values from -6 to 6
- pole_weight: float32 [4], P('pole'), may hold values from 0.25 to 1
- block_pattern: int32 [16, 16], replicated, may hold values 0 or 1
Outputs:
- density: float32 [4096, 4096], P('prow', 'pcol')
All inputs are finite; a program needn't handle non-finite values.
Results may differ from a plain program's by a relative error of at most 0.0001.
Values sent between devices are 32-bit elements; how exact they have to be, the bound alone decides.
A program may use at most 64 MiB of HBM per device.

v0:
```python
import jax
import jax.numpy as jnp
from jax import lax
from jax.sharding import PartitionSpec as P

B = 256


def tier_of(supers):
    halves = supers // 2
    upper_tier = jnp.where(halves < 4, 1, 2)
    return jnp.where(supers % 2 == 0, 0, upper_tier)


def node_of(supers):
    halves = supers // 2
    upper_node = jnp.where(halves < 4, halves // 2, 0)
    return jnp.where(supers % 2 == 0, halves // 2, upper_node)


def above(elders, youngers):
    tier_old = tier_of(elders)[:, None]
    tier_new = tier_of(youngers)[None, :]
    node_old = node_of(elders)[:, None]
    node_new = node_of(youngers)[None, :]
    shift_by = jnp.maximum(tier_old - tier_new, 0)
    return (tier_old > tier_new) & (node_old == jnp.right_shift(node_new, shift_by))


def same_node(firsts, seconds):
    tier_same = tier_of(firsts)[:, None] == tier_of(seconds)[None, :]
    node_same = node_of(firsts)[:, None] == node_of(seconds)[None, :]
    return tier_same & node_same


def highest(left, right):
    return jnp.dot(left, right, precision=lax.Precision.HIGHEST, preferred_element_type=jnp.float32)


def blockmul(values, mask):
    mask_rows, mask_cols = mask.shape
    shaped = values.reshape(
        mask_rows, values.shape[0] // mask_rows, mask_cols, values.shape[1] // mask_cols
    )
    return (shaped * mask[:, None, :, None].astype(values.dtype)).reshape(values.shape)


def quarter(values, row_slot, col_slot):
    height, breadth = values.shape
    shaped = values.reshape(height // (2 * B), 2, B, breadth // (2 * B), 2, B)
    return shaped[:, row_slot, :, :, col_slot, :].reshape(height // 2, breadth // 2)


def rows_in_slot(values, slot_now):
    height, breadth = values.shape
    return values.reshape(height // (2 * B), 2, B, breadth)[:, slot_now].reshape(
        height // 2, breadth
    )


def columns_in_slot(values, slot_now):
    height, breadth = values.shape
    return values.reshape(height, breadth // (2 * B), 2, B)[:, :, slot_now].reshape(
        height, breadth // 2
    )


def assemble(part_even, part_mixed, part_cross, part_odd):
    half_rows, half_cols = part_even.shape
    shape_four = (half_rows // B, B, half_cols // B, B)
    top_half = jnp.stack([part_even.reshape(shape_four), part_mixed.reshape(shape_four)], axis=3)
    bottom_half = jnp.stack([part_cross.reshape(shape_four), part_odd.reshape(shape_four)], axis=3)
    return jnp.stack([top_half, bottom_half], axis=1).reshape(2 * half_rows, 2 * half_cols)


def local(lower, upper, dinv, pole_weight, block_pattern):
    height, breadth = (lower.shape[1], lower.shape[2])
    row_blocks = height // B
    col_blocks = breadth // B
    row_sup = lax.axis_index("prow") * row_blocks + jnp.arange(row_blocks)
    col_sup = lax.axis_index("pcol") * col_blocks + jnp.arange(col_blocks)
    pattern_here = lax.dynamic_slice(
        block_pattern, (row_sup[0], col_sup[0]), (row_blocks, col_blocks)
    )
    pattern_flip = lax.dynamic_slice(
        block_pattern, (col_sup[0], row_sup[0]), (col_blocks, row_blocks)
    ).T
    keep_lower = above(row_sup, col_sup) & (pattern_here > 0)
    keep_upper = above(col_sup, row_sup).T & (pattern_flip > 0)
    row_odd = row_sup[1::2]
    col_odd = col_sup[1::2]
    root_mask = same_node(row_odd, col_odd) & (tier_of(row_odd)[:, None] == 2)
    empty = jnp.zeros((height // 2, breadth // 2), jnp.float32)
    weight = pole_weight[0]
    lmat = blockmul(lower[0], keep_lower)
    umat = blockmul(upper[0], keep_upper)
    lower_panel = lax.all_gather(rows_in_slot(lmat, 1), "prow", axis=0, tiled=True)
    upper_panel = lax.all_gather(columns_in_slot(umat, 1), "pcol", axis=1, tiled=True)
    greens_odd = blockmul(quarter(dinv[0], 1, 1), root_mask)
    panel = empty
    rowpart = empty
    diagpart = empty
    for tier_now in (1, 0):
        slot_now = 0 if tier_now == 0 else 1
        row_tier = row_sup[slot_now::2]
        col_tier = col_sup[slot_now::2]
        left_factor = columns_in_slot(lower_panel, slot_now)
        right_factor = rows_in_slot(upper_panel, slot_now)

        def along_columns(piece):
            return highest(right_factor, piece)

        folded_rows = highest(lax.all_gather(greens_odd, "pcol", axis=1, tiled=True), left_factor)
        col_flags = tier_of(col_tier) == tier_now
        row_flags = tier_of(row_tier) == tier_now
        panel = -blockmul(folded_rows, above(row_odd, col_tier) & col_flags[None, :])
        folded_columns = along_columns(lax.all_gather(greens_odd, "prow", axis=0, tiled=True))
        rowpart = -blockmul(folded_columns, above(col_odd, row_tier).T & row_flags[:, None])
        correction = along_columns(lax.all_gather(panel, "prow", axis=0, tiled=True))
        share = same_node(row_tier, col_tier) & row_flags[:, None]
        diagpart = blockmul(quarter(dinv[0], slot_now, slot_now) - correction, share)
        if tier_now > 0:
            greens_odd = greens_odd + panel + rowpart + diagpart
    density = weight * assemble(diagpart, rowpart, panel, greens_odd)
    return lax.psum(density, "pole")


def solution(mesh):
    in_specs = (
        P("pole", "prow", "pcol"),
        P("pole", "prow", "pcol"),
        P("pole", "prow", "pcol"),
        P("pole"),
        P(),
    )
    out_specs = P("prow", "pcol")
    return jax.shard_map(local, mesh=mesh, in_specs=in_specs, out_specs=out_specs, check_vma=False)
```

profile of v0, /device:TPU:1, one launch (start us, length us, event | category | flops | bytes accessed | tf_op | source)
XLA Modules:
  0.0 553.8 jit_solution(16048855129079267908)
XLA Ops:
  13.8 1.9 slice_multiply_fusion
  24.0 1.5 slice_multiply_fusion.1
  25.6 29.1 %all-gather.25.cloned.1.call-done = f32[1,1,2048,512]{3,2,1,0:T(8,128)} async-done(((f32[1,1,256,512]{3,2,1,0:T(8,128)}), f32[1,1,2048,512]{3,2,1,0:T(8,128)}) %all-gather.25.cloned.1.call-update) | async-done | bytes 4194320 | tf_op jit(solution)/shard_map/all_gather | solution.py:97
  54.7 5.9 %reshape.388 = f32[2048,1,2,256]{3,2,0,1:T(2,128)} reshape(f32[1,1,2048,512]{3,2,1,0:T(8,128)} %all-gather.25.cloned.1.call-done) | data formatting | bytes 8388608 | tf_op jit(solution)/shard_map/reshape | solution.py:63
  60.6 7.6 %fusion.69 = (f32[2048,1,1,256]{3,2,0,1:T(1,128)}, f32[2048,1,1,256]{3,2,0,1:T(1,128)S(1)}) fusion(f32[2048,1,2,256]{3,2,0,1:T(2,128)} %reshape.388), kind=kLoop, calls=%fused_computation.77 | loop fusion | bytes 8388608 | tf_op jit(solution)/shard_map/slice | solution.py:63
  68.2 64.3 %all-gather.11.cloned.1.call-done = f32[256,2048]{1,0:T(8,128)} async-done(((f32[256,256]{1,0:T(8,128)}), f32[256,2048]{1,0:T(8,128)}) %all-gather.11.cloned.1.call-update) | async-done | bytes 2097168 | tf_op jit(solution)/shard_map/all_gather | solution.py:113
  132.5 4.2 fusion.39
  137.6 144.1 %all-gather.23.cloned.1.call-done = f32[512,1,1,2048]{3,2,0,1:T(1,128)} async-done(((f32[512,1,1,256]{3,2,0,1:T(1,128)}), f32[512,1,1,2048]{3,2,0,1:T(1,128)}) %all-gather.23.cloned.1.call-update) | async-done | bytes 4194320 | tf_op jit(solution)/shard_map/all_gather | solution.py:98
  281.7 6.5 %fusion.68 = (f32[1,1,256,2048]{3,0,2,1:T(1,128)S(1)}, f32[1,1,256,2048]{3,0,2,1:T(1,128)}) fusion(f32[1,2,256,2048]{3,0,2,1:T(1,128)} %bitcast.118), kind=kLoop, calls=%fused_computation.76 | loop fusion | bytes 8388608 | tf_op jit(solution)/shard_map/slice | solution.py:56
  288.1 19.3 %all-gather.15.cloned.1.call-done = f32[2048,256]{1,0:T(8,128)} async-done(((f32[256,256]{1,0:T(8,128)}), f32[2048,256]{1,0:T(8,128)}) %all-gather.15.cloned.1.call-update) | async-done | bytes 2097168 | tf_op jit(solution)/shard_map/all_gather | solution.py:119
  307.4 4.6 fusion.57
  312.0 25.2 %all-gather.13.cloned.1.call-done = f32[2048,256]{1,0:T(8,128)} async-done(((f32[256,256]{1,0:T(8,128)}), f32[2048,256]{1,0:T(8,128)}) %all-gather.13.cloned.1.call-update) | async-done | bytes 2097168 | tf_op jit(solution)/shard_map/all_gather | solution.py:117
  337.2 5.2 fusion.51
  345.8 72.5 %all-gather.17.cloned.1.call-done = f32[256,2048]{1,0:T(8,128)} async-done(((f32[256,256]{1,0:T(8,128)}), f32[256,2048]{1,0:T(8,128)}) %all-gather.17.cloned.1.call-update) | async-done | bytes 2097168 | tf_op jit(solution)/shard_map/all_gather | solution.py:113
  418.3 4.9 fusion.63
  426.9 1.0 maximum_bitcast_fusion.1
  427.9 17.4 %all-gather.21.cloned.1.call-done = f32[2048,256]{1,0:T(8,128)} async-done(((f32[256,256]{1,0:T(8,128)}), f32[2048,256]{1,0:T(8,128)}) %all-gather.21.cloned.1.call-update) | async-done | bytes 2097168 | tf_op jit(solution)/shard_map/all_gather | solution.py:117
  445.3 3.9 fusion.33
  449.2 26.0 %all-gather.19.cloned.1.call-done = f32[2048,256]{1,0:T(8,128)} async-done(((f32[256,256]{1,0:T(8,128)}), f32[2048,256]{1,0:T(8,128)}) %all-gather.19.cloned.1.call-update) | async-done | bytes 2097168 | tf_op jit(solution)/shard_map/all_gather | solution.py:119
  475.2 3.9 fusion.24
  479.3 0.8 copy.20
  480.1 1.0 copy.30
  481.2 63.8 %all-reduce.2.cloned.1.call-done = f32[512,512]{1,0:T(8,128)} async-done(((f32[512,512]{1,0:T(8,128)}), f32[512,512]{1,0:T(8,128)}) %all-reduce.2.cloned.1.call-update) | async-done | bytes 1048592 | tf_op jit(solution)/shard_map/psum | solution.py:125
  545.0 2.3 copy.97
  (51 shorter events, 8.2 us)
Async XLA Ops:
  6.5 14.5 %copy-start.3 = (f32[1,512,512]{2,1,0:T(8,128)S(1)}, f32[1,512,512]{2,1,0:T(8,128)}, u32[]{:S(2)}) copy-start(f32[1,512,512]{2,1,0:T(8,128)} %param.7) | copy-start | bytes 3145732
  6.5 48.1 %all-gather.25.cloned.1.call-start = ((), (), s32[]{:S(2)}) async-start(), calls=%async_computation.8 | async-start | bytes 4718592 | tf_op jit(solution)/shard_map/all_gather | solution.py:97
  15.7 116.8 %all-gather.11.cloned.1.call-start = ((), (), s32[]{:S(2)}) async-start(), calls=%async_computation | async-start | bytes 2359296 | tf_op jit(solution)/shard_map/all_gather | solution.py:113
  21.7 1.5 copy-start.4
  23.0 258.7 %all-gather.23.cloned.1.call-start = ((), (), s32[]{:S(2)}) async-start(), calls=%async_computation.7 | async-start | bytes 4718592 | tf_op jit(solution)/shard_map/all_gather | solution.py:98
  25.5 281.9 %all-gather.15.cloned.1.call-start = ((), (), s32[]{:S(2)}) async-start(), calls=%async_computation.2 | async-start | bytes 2359296 | tf_op jit(solution)/shard_map/all_gather | solution.py:119
  136.7 200.5 %all-gather.13.cloned.1.call-start = ((), (), s32[]{:S(2)}) async-start(), calls=%async_computation.1 | async-start | bytes 2359296 | tf_op jit(solution)/shard_map/all_gather | solution.py:117
  137.3 280.9 %all-gather.17.cloned.1.call-start = ((), (), s32[]{:S(2)}) async-start(), calls=%async_computation.3 | async-start | bytes 2359296 | tf_op jit(solution)/shard_map/all_gather | solution.py:113
  307.4 29.8 %copy-start = (f32[256,256]{1,0:T(8,128)S(1)}, f32[256,256]{1,0:T(8,128)}, u32[]{:S(2)}) copy-start(f32[256,256]{1,0:T(8,128)} %fusion.66) | copy-start | bytes 786436
  307.4 29.8 %copy-start.2 = (f32[256,256]{1,0:T(8,128)S(1)}, f32[256,256]{1,0:T(8,128)}, u32[]{:S(2)}) copy-start(f32[256,256]{1,0:T(8,128)} %fusion.39) | copy-start | bytes 786436
  342.5 102.9 %all-gather.21.cloned.1.call-start = ((), (), s32[]{:S(2)}) async-start(), calls=%async_computation.5 | async-start | bytes 2359296 | tf_op jit(solution)/shard_map/all_gather | solution.py:117
  343.2 132.0 %all-gather.19.cloned.1.call-start = ((), (), s32[]{:S(2)}) async-start(), calls=%async_computation.4 | async-start | bytes 2359296 | tf_op jit(solution)/shard_map/all_gather | solution.py:119
  418.3 8.6 %copy-start.1 = (f32[256,256]{1,0:T(8,128)S(1)}, f32[256,256]{1,0:T(8,128)}, u32[]{:S(2)}) copy-start(f32[256,256]{1,0:T(8,128)} %fusion.51) | copy-start | bytes 786436
  423.2 121.9 %all-reduce.2.cloned.1.call-start = ((), (), s32[]{:S(2)}) async-start(), calls=%async_computation.6 | async-start | bytes 2097152 | tf_op jit(solution)/shard_map/psum | solution.py:125
Sparse Core Ops, SparseCore 0:
  15.8 38.8 all-gather.24
  57.2 75.3 all-gather.10
  135.0 146.6 all-gather.22
  283.4 24.0 all-gather.14
  309.1 28.0 all-gather.12
  342.6 75.6 all-gather.16
  420.1 25.1 all-gather.20
  447.2 28.0 all-gather.18
  481.3 63.6 all-reduce.1
where the time goes:
time: 555 us; the launch traced here: 554 us
  waiting for transfers between devices  463 us (83%)
  between operations  28.7 us (5%)
  local copies, waits for them, and re-layouts  27.7 us (5%)
  matrix products  26.7 us (5%)
  other arithmetic  6.91 us (1%)
    all_gather x1, waiting for transfers between devices, local(): lax.all_gather(columns_in_slot(umat, 1), 'pcol', axis=1, tiled=True)  144 us
    all_gather x2, waiting for transfers between devices, local(): lax.all_gather(greens_odd, 'pcol', axis=1, tiled=True)  137 us
    psum x1, waiting for transfers between devices, local(): return lax.psum(density, 'pole')  63.8 us
    all_gather x2, waiting for transfers between devices, local(): lax.all_gather(panel, 'prow', axis=0, tiled=True)  45.3 us
    all_gather x2, waiting for transfers between devices, local(): lax.all_gather(greens_odd, 'prow', axis=0, tiled=True)  42.6 us
    all_gather x1, waiting for transfers between devices, local(): lax.all_gather(rows_in_slot(lmat, 1), 'prow', axis=0, tiled=True)  29.1 us
    dot_general x6, matrix products, highest(): jnp.dot(left, right, precision=lax.Precision.HIGHEST, preferred_element_t...  26.7 us
  transfers between devices with their start and end apart: 9, of which 9 were waited for; matrix products, arithmetic and copies ran while one was open for 8% of the time, Pallas kernels for 0%

commit v1 on v0

--- a/solution.py
+++ b/solution.py
@@ -4,6 +4,11 @@
 from jax.sharding import PartitionSpec as P
 
 B = 256
+
+
+def group_streams(arr_in, row_axis):
+    v_next = jnp.sum(lax.all_gather(arr_in, row_axis), axis=0)
+    return v_next
 
 
 def tier_of(supers):
@@ -122,7 +127,7 @@
         if tier_now > 0:
             greens_odd = greens_odd + panel + rowpart + diagpart
     density = weight * assemble(diagpart, rowpart, panel, greens_odd)
-    return lax.psum(density, "pole")
+    return group_streams(density, "pole")
 
 
 def solution(mesh):

time: 555 us -> 577 us (1.040)
  waiting for transfers between devices: 463 us -> 483 us
    all_gather x0 -> x1, waiting for transfers between devices: none -> 84 us  [group_streams(): v_next = jnp.sum(lax.all_gather(arr_in, row_axis), axis=0)]
    psum x1 -> x0, waiting for transfers between devices: 63.8 us -> none  [local(): return lax.psum(density, 'pole')]
  transfers between devices with their start and end apart: 9 -> 9, of which waited for: 9 -> 9; matrix products, arithmetic and copies ran while one was open for 8% -> 7% of each run, Pallas kernels for 0% -> 0%
where the time goes in v1:
time: 577 us; the launch traced here: 576 us
  waiting for transfers between devices  483 us (84%)
  between operations  28.7 us (5%)
  matrix products  26.7 us (5%)
  local copies, waits for them, and re-layouts  26.2 us (5%)
  other arithmetic  10.6 us (2%)
    all_gather x1, waiting for transfers between devices, local(): lax.all_gather(columns_in_slot(umat, 1), 'pcol', axis=1, tiled=True)  144 us
    all_gather x2, waiting for transfers between devices, local(): lax.all_gather(greens_odd, 'pcol', axis=1, tiled=True)  137 us
    all_gather x1, waiting for transfers between devices, group_streams(): v_next = jnp.sum(lax.all_gather(arr_in, row_axis), axis=0)  84 us
    all_gather x2, waiting for transfers between devices, local(): lax.all_gather(panel, 'prow', axis=0, tiled=True)  45.3 us
    all_gather x2, waiting for transfers between devices, local(): lax.all_gather(greens_odd, 'prow', axis=0, tiled=True)  42.6 us
    all_gather x1, waiting for transfers between devices, local(): lax.all_gather(rows_in_slot(lmat, 1), 'prow', axis=0, tiled=True)  29.1 us
    dot_general x6, matrix products, highest(): jnp.dot(left, right, precision=lax.Precision.HIGHEST, preferred_element_t...  26.7 us
  transfers between devices with their start and end apart: 9, of which 9 were waited for; matrix products, arithmetic and copies ran while one was open for 7% of the time, Pallas kernels for 0%

profile of v1, /device:TPU:1, one launch (start us, length us, event | category | flops | bytes accessed | tf_op | source)
XLA Modules:
  0.0 576.2 jit_solution(8540137907187857277)
XLA Ops:
  13.8 1.9 slice_multiply_fusion
  24.0 1.5 slice_multiply_fusion.1
  25.6 29.1 %all-gather.28.cloned.1.call-done = f32[1,1,2048,512]{3,2,1,0:T(8,128)} async-done(((f32[1,1,256,512]{3,2,1,0:T(8,128)}), f32[1,1,2048,512]{3,2,1,0:T(8,128)}) %all-gather.28.cloned.1.call-update) | async-done | bytes 4194320 | tf_op jit(solution)/shard_map/all_gather | solution.py:102
  54.7 5.9 %reshape.398 = f32[2048,1,2,256]{3,2,0,1:T(2,128)} reshape(f32[1,1,2048,512]{3,2,1,0:T(8,128)} %all-gather.28.cloned.1.call-done) | data formatting | bytes 8388608 | tf_op jit(solution)/shard_map/reshape | solution.py:68
  60.6 7.6 %fusion.69 = (f32[2048,1,1,256]{3,2,0,1:T(1,128)}, f32[2048,1,1,256]{3,2,0,1:T(1,128)S(1)}) fusion(f32[2048,1,2,256]{3,2,0,1:T(2,128)} %reshape.398), kind=kLoop, calls=%fused_computation.77 | loop fusion | bytes 8388608 | tf_op jit(solution)/shard_map/slice | solution.py:68
  68.2 64.3 %all-gather.12.cloned.1.call-done = f32[256,2048]{1,0:T(8,128)} async-done(((f32[256,256]{1,0:T(8,128)}), f32[256,2048]{1,0:T(8,128)}) %all-gather.12.cloned.1.call-update) | async-done | bytes 2097168 | tf_op jit(solution)/shard_map/all_gather | solution.py:118
  132.5 4.2 fusion.39
  137.6 144.1 %all-gather.26.cloned.1.call-done = f32[512,1,1,2048]{3,2,0,1:T(1,128)} async-done(((f32[512,1,1,256]{3,2,0,1:T(1,128)}), f32[512,1,1,2048]{3,2,0,1:T(1,128)}) %all-gather.26.cloned.1.call-update) | async-done | bytes 4194320 | tf_op jit(solution)/shard_map/all_gather | solution.py:103
  281.7 6.5 %fusion.68 = (f32[1,1,256,2048]{3,0,2,1:T(1,128)S(1)}, f32[1,1,256,2048]{3,0,2,1:T(1,128)}) fusion(f32[1,2,256,2048]{3,0,2,1:T(1,128)} %bitcast.116), kind=kLoop, calls=%fused_computation.76 | loop fusion | bytes 8388608 | tf_op jit(solution)/shard_map/slice | solution.py:61
  288.1 19.3 %all-gather.16.cloned.1.call-done = f32[2048,256]{1,0:T(8,128)} async-done(((f32[256,256]{1,0:T(8,128)}), f32[2048,256]{1,0:T(8,128)}) %all-gather.16.cloned.1.call-update) | async-done | bytes 2097168 | tf_op jit(solution)/shard_map/all_gather | solution.py:124
  307.4 4.6 fusion.57
  312.0 25.2 %all-gather.14.cloned.1.call-done = f32[2048,256]{1,0:T(8,128)} async-done(((f32[256,256]{1,0:T(8,128)}), f32[2048,256]{1,0:T(8,128)}) %all-gather.14.cloned.1.call-update) | async-done | bytes 2097168 | tf_op jit(solution)/shard_map/all_gather | solution.py:122
  337.2 5.2 fusion.51
  345.8 72.5 %all-gather.18.cloned.1.call-done = f32[256,2048]{1,0:T(8,128)} async-done(((f32[256,256]{1,0:T(8,128)}), f32[256,2048]{1,0:T(8,128)}) %all-gather.18.cloned.1.call-update) | async-done | bytes 2097168 | tf_op jit(solution)/shard_map/all_gather | solution.py:118
  418.3 4.9 fusion.63
  426.9 1.0 maximum_bitcast_fusion.1
  427.9 17.4 %all-gather.22.cloned.1.call-done = f32[2048,256]{1,0:T(8,128)} async-done(((f32[256,256]{1,0:T(8,128)}), f32[2048,256]{1,0:T(8,128)}) %all-gather.22.cloned.1.call-update) | async-done | bytes 2097168 | tf_op jit(solution)/shard_map/all_gather | solution.py:122
  445.3 3.9 fusion.33
  449.2 26.0 %all-gather.20.cloned.1.call-done = f32[2048,256]{1,0:T(8,128)} async-done(((f32[256,256]{1,0:T(8,128)}), f32[2048,256]{1,0:T(8,128)}) %all-gather.20.cloned.1.call-update) | async-done | bytes 2097168 | tf_op jit(solution)/shard_map/all_gather | solution.py:124
  475.2 3.9 fusion.24
  479.3 0.8 copy.29
  480.1 1.8 mul.195
  482.0 84.0 %all-gather.24.cloned.1.call-done = f32[4,512,512]{2,1,0:T(8,128)} async-done(((f32[1,512,512]{2,1,0:T(8,128)}), f32[4,512,512]{2,1,0:T(8,128)}) %all-gather.24.cloned.1.call-update) | async-done | bytes 4194320 | tf_op jit(solution)/shard_map/all_gather | solution.py:10
  566.0 3.7 reduce_sum.9
  (51 shorter events, 8.2 us)
Async XLA Ops:
  6.5 14.5 %copy-start.3 = (f32[1,512,512]{2,1,0:T(8,128)S(1)}, f32[1,512,512]{2,1,0:T(8,128)}, u32[]{:S(2)}) copy-start(f32[1,512,512]{2,1,0:T(8,128)} %param.7) | copy-start | bytes 3145732
  6.5 48.1 %all-gather.28.cloned.1.call-start = ((), (), s32[]{:S(2)}) async-start(), calls=%async_computation.8 | async-start | bytes 4718592 | tf_op jit(solution)/shard_map/all_gather | solution.py:102
  15.7 116.8 %all-gather.12.cloned.1.call-start = ((), (), s32[]{:S(2)}) async-start(), calls=%async_computation | async-start | bytes 2359296 | tf_op jit(solution)/shard_map/all_gather | solution.py:118
  21.7 1.5 copy-start.4
  23.0 258.7 %all-gather.26.cloned.1.call-start = ((), (), s32[]{:S(2)}) async-start(), calls=%async_computation.7 | async-start | bytes 4718592 | tf_op jit(solution)/shard_map/all_gather | solution.py:103
  25.5 281.9 %all-gather.16.cloned.1.call-start = ((), (), s32[]{:S(2)}) async-start(), calls=%async_computation.2 | async-start | bytes 2359296 | tf_op jit(solution)/shard_map/all_gather | solution.py:124
  136.7 200.5 %all-gather.14.cloned.1.call-start = ((), (), s32[]{:S(2)}) async-start(), calls=%async_computation.1 | async-start | bytes 2359296 | tf_op jit(solution)/shard_map/all_gather | solution.py:122
  137.3 280.9 %all-gather.18.cloned.1.call-start = ((), (), s32[]{:S(2)}) async-start(), calls=%async_computation.3 | async-start | bytes 2359296 | tf_op jit(solution)/shard_map/all_gather | solution.py:118
  307.4 29.8 %copy-start = (f32[256,256]{1,0:T(8,128)S(1)}, f32[256,256]{1,0:T(8,128)}, u32[]{:S(2)}) copy-start(f32[256,256]{1,0:T(8,128)} %fusion.66) | copy-start | bytes 786436
  307.4 29.8 %copy-start.2 = (f32[256,256]{1,0:T(8,128)S(1)}, f32[256,256]{1,0:T(8,128)}, u32[]{:S(2)}) copy-start(f32[256,256]{1,0:T(8,128)} %fusion.39) | copy-start | bytes 786436
  342.5 102.9 %all-gather.22.cloned.1.call-start = ((), (), s32[]{:S(2)}) async-start(), calls=%async_computation.5 | async-start | bytes 2359296 | tf_op jit(solution)/shard_map/all_gather | solution.py:122
  343.2 132.0 %all-gather.20.cloned.1.call-start = ((), (), s32[]{:S(2)}) async-start(), calls=%async_computation.4 | async-start | bytes 2359296 | tf_op jit(solution)/shard_map/all_gather | solution.py:124
  418.3 8.6 %copy-start.1 = (f32[256,256]{1,0:T(8,128)S(1)}, f32[256,256]{1,0:T(8,128)}, u32[]{:S(2)}) copy-start(f32[256,256]{1,0:T(8,128)} %fusion.51) | copy-start | bytes 786436
  423.2 142.8 %all-gather.24.cloned.1.call-start = ((), (), s32[]{:S(2)}) async-start(), calls=%async_computation.6 | async-start | bytes 5242880 | tf_op jit(solution)/shard_map/all_gather | solution.py:10
Sparse Core Ops, SparseCore 0:
  15.8 38.8 all-gather.27
  57.2 75.3 all-gather.11
  135.0 146.6 all-gather.25
  283.4 24.0 all-gather.15
  309.1 28.0 all-gather.13
  342.6 75.6 all-gather.17
  420.1 25.1 all-gather.21
  447.2 28.0 all-gather.19
  482.1 83.8 all-gather.23
